TPU v7x, 32 devices: a whole 2x2x4 slice. The times are simulated.
32 devices in a mesh: groups: 2 (over x), hid: 8 (over z, y), ffn: 2 (over core).
Axes of the slice: x: 2, y: 2, z: 4, core: 2. Of those that a mesh axis runs over, the one named last changes fastest.
Arguments:
- hidden_in: bfloat16 [192, 16384], P('groups', 'hid'), parts along dimension 0, may hold values from -6 to 6
- w_query: bfloat16 [16384, 8192], P('hid', 'ffn'), may hold values from -0.046875 to 0.046875
- w_key: bfloat16 [16384, 512], P('hid', 'ffn'), may hold values from -0.046875 to 0.046875
- w_value: bfloat16 [16384, 512], P('hid', 'ffn'), may hold values from -0.046875 to 0.046875
- w_out: bfloat16 [8192, 16384], P('ffn', 'hid'), may hold values from -0.25 to 0.25
- key_cache: bfloat16 [192, 256, 4, 128], P(('groups', 'hid'), None, 'ffn'), parts along dimension 0
- value_cache: bfloat16 [192, 256, 4, 128], P(('groups', 'hid'), None, 'ffn'), parts along dimension 0, may hold values from -6 to 6
- lengths: int32 [192], P(('groups', 'hid')), parts along dimension 0, may hold values from 1 to 256, as said below
- slot_pos: int32 [192, 256], P(('groups', 'hid')), parts along dimension 0, may hold values from 0 to 255, each once within a row
Outputs:
- block_out: bfloat16 [192, 16384], P(('groups', 'ffn'), 'hid'), parts along dimension 0
There are 2 independent parts, one for each index of `groups`. A program takes and returns all parts, laid end to end along the dimension named above; an argument that names none is the same for every part. Nothing has to cross between parts.
Inputs may be any that keep to these rules, and one draw needn't show every extreme that they name: `slot_pos`: each row of a request's slots holds every position 0 to 255 exactly once. `lengths`: some request has exactly 256 earlier tokens.
All inputs are finite; a program needn't handle non-finite values.
Results may differ from a plain program's by a relative error of at most 0.012.
Values may be sent and summed in bfloat16 or wider, within the bound.
A program may use at most 128 MiB of HBM per device.

v0:
```python
import jax
import jax.numpy as jnp
from jax import lax
from jax.sharding import PartitionSpec as P

HD = 128


def rotate(tensor, pos):
    half = tensor.shape[-1] // 2
    freq = 500000.0 ** (-(jnp.arange(half, dtype=jnp.float32) * 2.0) / tensor.shape[-1])
    angle = pos[:, None, None] * freq[None, None, :]
    cosine = jnp.cos(angle)
    sine = jnp.sin(angle)
    first = tensor[..., :half]
    second = tensor[..., half:]
    return jnp.concatenate(
        [first * cosine - second * sine, second * cosine + first * sine], axis=-1
    )


def per_device(
    hidden_in, w_query, w_key, w_value, w_out, key_cache, value_cache, lengths, slot_pos
):
    rows = key_cache.shape[0]
    heads_here = w_query.shape[1] // HD
    kv_here = w_key.shape[1] // HD
    group = heads_here // kv_here
    query_cols = w_query.shape[1]
    kv_cols = w_key.shape[1]
    summed = lax.psum_scatter(
        jnp.concatenate(
            [
                jnp.dot(hidden_in, w_query, preferred_element_type=jnp.float32),
                jnp.dot(hidden_in, w_key, preferred_element_type=jnp.float32),
                jnp.dot(hidden_in, w_value, preferred_element_type=jnp.float32),
            ],
            axis=1,
        ),
        "hid",
        scatter_dimension=0,
        tiled=True,
    )
    query = summed[:, :query_cols]
    new_key = summed[:, query_cols : query_cols + kv_cols]
    new_value = summed[:, query_cols + kv_cols :]
    pos = lengths.astype(jnp.float32)
    rot_query = rotate(query.reshape(rows, heads_here, HD), pos).astype(jnp.bfloat16)
    rot_key = rotate(new_key.reshape(rows, kv_here, HD), pos).astype(jnp.bfloat16)
    value_b = new_value.reshape(rows, kv_here, HD).astype(jnp.bfloat16)
    scale = 1.0 / jnp.sqrt(jnp.float32(HD))
    grouped = rot_query.reshape(rows, kv_here, group, HD)
    scores = (
        jnp.einsum("rgjd,rtgd->rgjt", grouped, key_cache, preferred_element_type=jnp.float32)
        * scale
    )
    live = slot_pos < lengths[:, None]
    scores = jnp.where(live[:, None, None, :], scores, -jnp.inf)
    own = jnp.einsum("rgjd,rgd->rgj", grouped, rot_key, preferred_element_type=jnp.float32) * scale
    top = jnp.maximum(jnp.max(scores, axis=-1), own)
    expo = jnp.exp(scores - top[..., None])
    own_expo = jnp.exp(own - top)
    total = jnp.sum(expo, axis=-1) + own_expo
    weights = (expo / total[..., None]).astype(jnp.bfloat16)
    own_weight = (own_expo / total).astype(jnp.bfloat16)
    attended = jnp.einsum(
        "rgjt,rtgd->rgjd", weights, value_cache, preferred_element_type=jnp.float32
    )
    attended = (
        attended
        + own_weight.astype(jnp.float32)[..., None] * value_b.astype(jnp.float32)[:, :, None, :]
    )
    attended = attended.reshape(rows, heads_here * HD).astype(jnp.bfloat16)
    terms = jnp.dot(
        lax.all_gather(attended, "hid", axis=0, tiled=True),
        w_out,
        preferred_element_type=jnp.float32,
    )
    return lax.psum_scatter(terms, "ffn", scatter_dimension=0, tiled=True).astype(jnp.bfloat16)


def solution(mesh):
    placed = (
        P("groups", "hid"),
        P("hid", "ffn"),
        P("hid", "ffn"),
        P("hid", "ffn"),
        P("ffn", "hid"),
        P(("groups", "hid"), None, "ffn", None),
        P(("groups", "hid"), None, "ffn", None),
        P(("groups", "hid")),
        P(("groups", "hid"), None),
    )
    return jax.shard_map(
        per_device,
        mesh=mesh,
        in_specs=placed,
        out_specs=P(("groups", "ffn"), "hid"),
        check_vma=False,
    )
```

profile of v0, /device:TPU:0, one launch (start us, length us, event | category | flops | bytes accessed | tf_op | source)
XLA Modules:
  0.0 178.8 jit_solution(15094963762838237554)
XLA Ops:
  6.6 8.8 %fusion.27 = f32[96,4096]{1,0:T(8,128)S(1)} fusion(bf16[96,2048]{1,0:T(8,128)(2,1)} %param.9, bf16[2048,4096]{1,0:T(8,128)(2,1)} %param.10), kind=kOutput, calls=%fused_computation.37 | convolution fusion | flops 1610612736 | bytes 18743296 | tf_op jit(solution)/shard_map/dot_general | solution.py:34
  15.4 0.3 fusion.28
  15.7 0.3 fusion.29
  16.0 1.3 pad_maximum_fusion
  17.4 0.6 copy-done.5
  18.0 0.6 dynamic-slice
  19.3 0.1 multiply_cosine_fusion
  19.5 94.3 %all-reduce.3.cloned.1.call-done = f32[96,4608]{1,0:T(8,128)} async-done(((f32[96,4608]{1,0:T(8,128)}), f32[96,4608]{1,0:T(8,128)}) %all-reduce.3.cloned.1.call-update) | async-done | bytes 1769488
  113.8 0.8 dynamic-slice.3
  114.6 1.0 constant_dynamic-slice_fusion
  115.8 0.1 subtract_convert_fusion.1
  115.8 0.1 subtract_convert_fusion
  116.0 0.1 maximum_bitcast_fusion
  116.1 0.2 fusion.19
  116.3 0.7 fusion.26
  117.0 0.3 fusion.16
  117.3 0.8 fusion.21
  118.1 1.8 %fusion.13 = bf16[12,2,16,128]{3,2,1,0:T(8,128)(2,1)S(1)} fusion(bf16[12,256,2,128]{3,2,1,0:T(2,128)(2,1)} %param.15, f32[12,2,16,256]{3,2,1,0:T(8,128)S(1)} %get-tuple-element.14, f32[12,2,16]{2,1,0:T(2,128)S(1)} %get-tuple-element.8, f32[12,2,16]{2,1,0:T(2,128)S(1)} %multiply_maximum_fusion, f32[12,2,128]{2,1,0:T(2,128)S(1)} %reshape.91, ...), kind=kOutput, calls=%fused_computation.8 | convolution fusion | flops 25608192 | bytes 2081280 | tf_op jit(solution)/shard_map/rgjt,rtgd->rgjd/dot_general | solution.py:66
  119.9 0.1 reshape.92
  120.0 32.7 %all-gather = bf16[8,12,4096]{2,1,0:T(8,128)(2,1)S(1)} all-gather(bf16[1,12,4096]{2,1,0:T(8,128)(2,1)S(1)} %reshape.92), channel_id=1, replica_groups=mesh['groups'=2,'hid'=8,'ffn'=2] {'hid'}, dimensions={0}, use_global_device_ids=true | all-gather | bytes 884736 | tf_op jit(solution)/shard_map/all_gather | solution.py:75
  152.8 0.2 reshape.93
  152.9 9.4 %fusion.30 = f32[96,2048]{1,0:T(8,128)} fusion(bf16[96,4096]{1,0:T(8,128)(2,1)S(1)} %reshape.93, bf16[4096,2048]{1,0:T(8,128)(2,1)} %param.13), kind=kOutput, calls=%fused_computation.40 | convolution fusion | flops 1610612736 | bytes 18350080 | tf_op jit(solution)/shard_map/dot_general | solution.py:74
  162.4 7.9 %reduce-scatter.2.cloned.1.call-done = f32[48,2048]{1,0:T(8,128)} async-done(((f32[96,2048]{1,0:T(8,128)}), f32[48,2048]{1,0:T(8,128)}) %reduce-scatter.2.cloned.1.call-update) | async-done | bytes 393232 | tf_op jit(solution)/shard_map/reduce_scatter | solution.py:79
  170.2 1.7 convert_element_type.48
  (26 shorter events, 0.3 us)
Async XLA Ops:
  6.5 109.8 %copy-start = (bf16[12,256,2,128]{3,2,1,0:T(2,128)(2,1)S(1)}, bf16[12,256,2,128]{3,2,1,0:T(2,128)(2,1)}, u32[]{:S(2)}) copy-start(bf16[12,256,2,128]{3,2,1,0:T(2,128)(2,1)} %param.14) | copy-start | bytes 4718596
  6.5 8.8 %copy-start.1 = (bf16[96,2048]{1,0:T(8,128)(2,1)S(1)}, bf16[96,2048]{1,0:T(8,128)(2,1)}, u32[]{:S(2)}) copy-start(bf16[96,2048]{1,0:T(8,128)(2,1)} %param.9) | copy-start | bytes 1179652
  6.5 8.8 %copy-start.2 = (bf16[2048,256]{1,0:T(8,128)(2,1)S(1)}, bf16[2048,256]{1,0:T(8,128)(2,1)}, u32[]{:S(2)}) copy-start(bf16[2048,256]{1,0:T(8,128)(2,1)} %param.11) | copy-start | bytes 3145732
  6.5 107.2 %all-reduce.3.cloned.1.call-start = ((), (), s32[]{:S(2)}) async-start(), calls=%async_computation.2 | async-start | bytes 3538944
  6.5 9.1 %copy-start.3 = (bf16[2048,256]{1,0:T(8,128)(2,1)S(1)}, bf16[2048,256]{1,0:T(8,128)(2,1)}, u32[]{:S(2)}) copy-start(bf16[2048,256]{1,0:T(8,128)(2,1)} %param.12) | copy-start | bytes 3145732
  17.3 0.7 copy-start.5
  17.4 0.7 copy-start.6
  17.4 2.0 %copy-start.4 = (s32[12,256]{1,0:T(8,128)S(1)}, s32[12,256]{1,0:T(8,128)}, u32[]{:S(2)}) copy-start(s32[12,256]{1,0:T(8,128)} %param.17) | copy-start | bytes 36868
  17.4 152.9 %reduce-scatter.2.cloned.1.call-start = ((), (), s32[]{:S(2)}) async-start(), calls=%async_computation.1 | async-start | bytes 1179648 | tf_op jit(solution)/shard_map/reduce_scatter | solution.py:79
Sparse Core Ops, SparseCore 0:
  17.5 96.2 all-reduce.2
  162.5 7.6 reduce-scatter.1
where the time goes:
time: 179 us
  waiting for transfers between devices  102 us (57%)
  blocking collectives  32.7 us (18%)
  matrix products  21.5 us (12%)
  between operations  14.2 us (8%)
  other arithmetic  4.65 us (3%)
  local copies, waits for them, and re-layouts  3.41 us (2%)
    unnamed x3, waiting for transfers between devices  94.3 us
    all_gather x1, blocking collectives, per_device(): lax.all_gather(attended, 'hid', axis=0, tiled=True)  32.7 us
    dot_general x1, matrix products, per_device(): jnp.dot(lax.all_gather(attended, 'hid', axis=0, tiled=True), w_out, prefe...  9.43 us
    dot_general x1, matrix products, per_device(): jnp.dot(hidden_in, w_query, preferred_element_type=jnp.float32)  8.79 us
    reduce_scatter x1, waiting for transfers between devices, per_device(): lax.psum_scatter(terms, 'ffn', scatter_dimension=0, tiled=True)  7.86 us
  transfers between devices with their start and end apart: 2, of which 2 were waited for; matrix products, arithmetic and copies ran while one was open for 0% of the time, Pallas kernels for 0%

commit v1 on v0

v1 whole, which is shorter than its diff:
```python
import functools
import math

import jax
import jax.numpy as jnp
from jax import lax
from jax.experimental import pallas as pl
from jax.experimental.pallas import tpu as pltpu
from jax.sharding import PartitionSpec as P

HD = 128
NH = 8
MESH = pl.DeviceIdType.MESH
F32 = jnp.float32
BF16 = jnp.bfloat16


def kernel(
    nb,
    len_ref, slot_ref, x_hbm, wq_hbm, wk_hbm, wv_hbm, wo_hbm, kc_hbm, vc_hbm,
    out_ref,
    x, wq, wkv, wo, kc, vc,
    fkv, fq, skv, sq, rkv, rq,
    cos_s, sin_s, qf, kvf, sc, of, ag, lf, lhs, acc, fin,
    local_sem, rs_send, rs_recv, ag_send, ag_recv, fin_send, fin_recv,
):
    hid = 1 << nb
    h = lax.axis_index("hid")
    f = lax.axis_index("ffn")
    my = [lax.rem(lax.div(h, 1 << b), 2) for b in range(nb)]
    partner = [h + (1 - 2 * my[b]) * (1 << b) for b in range(nb)]
    rows = x.shape[0]
    rb = rows // hid
    nq = wq.shape[0]
    qw = wq.shape[2]
    order = tuple(range(nb))

    cp_x = pltpu.make_async_copy(x_hbm, x, local_sem.at[0])
    cp_k = pltpu.make_async_copy(wk_hbm, wkv.at[0], local_sem.at[1])
    cp_v = pltpu.make_async_copy(wv_hbm, wkv.at[1], local_sem.at[2])
    cp_kc = pltpu.make_async_copy(kc_hbm, kc, local_sem.at[3])
    cp_vc = pltpu.make_async_copy(vc_hbm, vc, local_sem.at[4])
    cp_q = [
        pltpu.make_async_copy(wq_hbm.at[:, pl.ds(c * qw, qw)], wq.at[c], local_sem.at[5 + c])
        for c in range(nq)
    ]
    cp_o = [
        pltpu.make_async_copy(
            wo_hbm.at[pl.ds(c * qw, qw), :], wo.at[c], local_sem.at[5 + nq + c]
        )
        for c in range(nq)
    ]
    cp_x.start()
    cp_k.start()
    cp_v.start()
    cp_q[0].start()
    cp_q[1].start()

    barrier = pltpu.get_barrier_semaphore()
    for b in range(nb):
        pl.semaphore_signal(barrier, inc=1, device_id={"hid": partner[b]}, device_id_type=MESH)
    pl.semaphore_signal(barrier, inc=1, device_id={"ffn": 1 - f}, device_id_type=MESH)

    lane = lax.broadcasted_iota(jnp.int32, (1, HD), 1)
    idx = jnp.where(lane < HD // 2, lane, lane - HD // 2).astype(F32)
    freq = jnp.exp(idx * (-2.0 * math.log(500000.0) / HD))
    for r in range(rb):
        cos_s[r : r + 1, :] = len_ref[r].astype(F32) * freq
    angle = cos_s[...]
    sign = jnp.where(lane < HD // 2, -1.0, 1.0).astype(F32)
    sin_s[...] = jnp.sin(angle) * sign
    cos_s[...] = jnp.cos(angle)

    def bufs(c):
        if c == 0:
            return fkv, skv, rkv, rb * 4
        return fq.at[c - 1], sq.at[c - 1], rq.at[c - 1], rb * NH

    def rs_copy(c, k):
        _, s, r, block = bufs(c)
        count = hid >> (k + 1)
        start = hid - (hid >> k)
        part = pl.ds(start * block, count * block)
        return pltpu.make_async_remote_copy(
            src_ref=s.at[part], dst_ref=r.at[part],
            send_sem=rs_send.at[c * nb + k], recv_sem=rs_recv.at[c * nb + k],
            device_id={"hid": partner[order[k]]}, device_id_type=MESH,
        )

    def rs_stage(c, k):
        sums, s, r, block = bufs(c)
        if k > 0:
            rs_copy(c, k - 1).wait_recv()
        left = nb - k - 1
        start = hid - (hid >> k)
        before = hid - (hid >> (k - 1)) if k > 0 else 0
        base = 0
        for j in range(k):
            base = base + my[order[j]] * (1 << order[j])

        def at(i, bit):
            off = 0
            for m in range(left):
                off += ((i >> (left - 1 - m)) & 1) << order[k + 1 + m]
            t = base + bit * (1 << order[k]) + off
            return pl.ds(pl.multiple_of(t * block, block), block)

        def came(i, bit):
            p = before + bit * (1 << left) + i
            return pl.ds(pl.multiple_of(p * block, block), block)

        mine = my[order[k]]
        for i in range(1 << left):
            value = sums[at(i, 1 - mine), :]
            if k > 0:
                value = value + r[came(i, 1 - mine), :].astype(F32)
            s[pl.ds((start + i) * block, block), :] = value.astype(BF16)
        rs_copy(c, k).start()
        if k > 0:
            for i in range(1 << left):
                sums[at(i, mine), :] = sums[at(i, mine), :] + r[came(i, mine), :].astype(F32)

    def rs_final(c):
        sums, s, r, block = bufs(c)
        rs_copy(c, nb - 1).wait_recv()
        own = pl.ds(pl.multiple_of(h * block, block), block)
        value = sums[own, :] + r[pl.ds((hid - 2) * block, block), :].astype(F32)
        if c == 0:
            kvf[...] = value
            return
        value = value.reshape(rb, NH, HD)
        turned = pltpu.roll(value.reshape(rb * NH, HD), HD // 2, 1).reshape(rb, NH, HD)
        cosine = cos_s[...][:, None, :]
        sine = sin_s[...][:, None, :]
        qf[:, (c - 1) * NH : c * NH, :] = value * cosine + turned * sine

    cp_x.wait()
    for part, cp in ((0, cp_k), (1, cp_v)):
        cp.wait()
        got = jnp.dot(x[...], wkv[part], preferred_element_type=F32)
        for j in range(2):
            fkv[pl.ds(part * 2 + j, rows, stride=4), :] = got[:, j * HD : (j + 1) * HD]
    pl.semaphore_wait(barrier, nb + 1)
    rs_stage(0, 0)

    wave = []
    for c in range(nq):
        cp_q[c].wait()
        if c + 2 < nq:
            cp_q[c + 2].start()
        elif c + 2 == nq:
            cp_kc.start()
            cp_vc.start()
            cp_o[0].start()
        else:
            for o in range(1, nq):
                cp_o[o].start()

        @pl.loop(0, qw // 256)
        def _(n):
            cols = pl.ds(pl.multiple_of(n * 256, 256), 256)
            got = jnp.dot(x[...], wq.at[c][:, cols], preferred_element_type=F32)
            for j in range(2):
                fq.at[c][pl.ds(n * 2 + j, rows, stride=NH), :] = got[:, j * HD : (j + 1) * HD]

        rs_stage(c + 1, 0)
        if c > 0:
            rs_stage(c - 1, 1)

    done = {(c, 0) for c in range(nq + 1)} | {(c, 1) for c in range(nq - 1)}
    for w in range(nq + 1 + nb):
        for k in range(nb, 0, -1):
            c = w - k
            if 0 <= c <= nq and (c, k) not in done:
                if k == nb:
                    rs_final(c)
                else:
                    rs_stage(c, k)

    heads = nq * NH
    slots = slot_ref.shape[1]
    spread = (
        lax.broadcasted_iota(jnp.int32, (slots, 2 * slots), 0)
        == lax.div(lax.broadcasted_iota(jnp.int32, (slots, 2 * slots), 1), 2)
    )
    spread = jnp.where(spread, 1.0, 0.0).astype(BF16)
    position = jnp.dot(
        slot_ref[...].astype(F32).astype(BF16), spread, preferred_element_type=F32
    )
    parity = (
        lax.rem(lax.broadcasted_iota(jnp.int32, (heads, 2 * slots), 1), 2)
        == lax.div(lax.broadcasted_iota(jnp.int32, (heads, 2 * slots), 0), heads // 2)
    )
    scale = 1.0 / math.sqrt(HD)
    cp_kc.wait()
    cp_vc.wait()
    for r in range(rb):
        sc[r] = lax.dot_general(
            qf[r].astype(BF16), kc[r], (((1,), (1,)), ((), ())), preferred_element_type=F32
        )
    kvrot = kvf[...]
    turned = pltpu.roll(kvrot, HD // 2, 1)
    for r in range(rb):
        def both(first, second):
            return jnp.concatenate(
                [
                    jnp.broadcast_to(first, (heads // 2, HD)),
                    jnp.broadcast_to(second, (heads // 2, HD)),
                ],
                axis=0,
            )

        cosine = cos_s[r : r + 1, :]
        sine = sin_s[r : r + 1, :]
        key = [
            (kvrot[r * 4 + g : r * 4 + g + 1] * cosine + turned[r * 4 + g : r * 4 + g + 1] * sine)
            for g in range(2)
        ]
        key = both(*key).astype(BF16).astype(F32)
        value = both(kvrot[r * 4 + 2 : r * 4 + 3], kvrot[r * 4 + 3 : r * 4 + 4])
        value = value.astype(BF16).astype(F32)
        query = qf[r].astype(BF16).astype(F32)
        own = jnp.sum(query * key, axis=-1, keepdims=True) * scale
        live = position[r : r + 1, :] < len_ref[r].astype(F32)
        scores = jnp.where(live & parity, sc[r] * scale, -jnp.inf)
        top = jnp.maximum(jnp.max(scores, axis=-1, keepdims=True), own)
        expo = jnp.exp(scores - top)
        own_expo = jnp.exp(own - top)
        over = 1.0 / (jnp.sum(expo, axis=-1, keepdims=True) + own_expo)
        weights = (expo * over).astype(BF16)
        own_weight = (own_expo * over).astype(BF16).astype(F32)
        got = jnp.dot(weights, vc[r], preferred_element_type=F32) + own_weight * value
        for c in range(nq):
            of[c, r * NH : (r + 1) * NH, :] = got[c * NH : (c + 1) * NH]

    block = rb * NH
    place = 0
    for k in range(nb):
        place = place * 2 + my[order[k]]

    def ag_copy(c, k):
        start = lax.div(place, 1 << k) * (1 << k)
        part = pl.ds(pl.multiple_of(start * block, block), (1 << k) * block)
        return pltpu.make_async_remote_copy(
            src_ref=ag.at[c, part], dst_ref=ag.at[c, part],
            send_sem=ag_send.at[c * nb + k], recv_sem=ag_recv.at[c * nb + k],
            device_id={"hid": partner[order[nb - 1 - k]]}, device_id_type=MESH,
        )

    def position_of(t):
        p = 0
        for k in range(nb):
            p = p * 2 + ((t >> order[k]) & 1)
        return p

    half = rows // 2
    cols_out = out_ref.shape[1]
    tile = 512 if cols_out % 512 == 0 else cols_out
    tiles = cols_out // tile

    def fin_copy(n):
        cols = pl.ds(n * tile, tile)
        return pltpu.make_async_remote_copy(
            src_ref=acc.at[pl.ds(pl.multiple_of((1 - f) * half, half), half), cols],
            dst_ref=fin.at[:, cols],
            send_sem=fin_send.at[n], recv_sem=fin_recv.at[n],
            device_id={"ffn": 1 - f}, device_id_type=MESH,
        )

    def project(c):
        for t in range(hid):
            lf[t * block : (t + 1) * block, :] = ag[
                c, position_of(t) * block : (position_of(t) + 1) * block, :
            ].astype(F32)
        for j in range(NH):
            lhs[:, j * HD : (j + 1) * HD] = lf[pl.ds(j, rows, stride=NH), :].astype(BF16)
        cp_o[c].wait()
        for n in range(tiles):
            cols = pl.ds(n * tile, tile)
            got = jnp.dot(lhs[...], wo.at[c][:, cols], preferred_element_type=F32)
            if c == 0:
                acc[:, cols] = got
            else:
                acc[:, cols] = acc[:, cols] + got
            if c == nq - 1:
                fin_copy(n).start()

    for c in range(nq):
        own = pl.ds(pl.multiple_of(place * block, block), block)
        ag[c, own, :] = of[c].astype(BF16)
        ag_copy(c, 0).start()
    for w in range(1, nq + nb):
        for k in range(nb, 0, -1):
            c = w - k
            if 0 <= c < nq:
                ag_copy(c, k - 1).wait_recv()
                if k < nb:
                    ag_copy(c, k).start()
        c = w - nb
        if 0 <= c < nq:
            project(c)

    kept = pl.ds(pl.multiple_of(f * half, half), half)
    for n in range(tiles):
        cols = pl.ds(n * tile, tile)
        fin_copy(n).wait_recv()
        out_ref[:, cols] = (acc[kept, cols] + fin[:, cols]).astype(BF16)

    for c in range(nq + 1):
        for k in range(nb):
            rs_copy(c, k).wait_send()
    for c in range(nq):
        for k in range(nb):
            ag_copy(c, k).wait_send()
    for n in range(tiles):
        fin_copy(n).wait_send()


def per_device(hid, x, w_query, w_key, w_value, w_out, key_cache, value_cache, lengths, slot_pos):
    nb = hid.bit_length() - 1
    rows, depth = x.shape
    rb, slots, kvh, _ = key_cache.shape
    qcols = w_query.shape[1]
    qw = NH * HD
    nq = qcols // qw
    ncols = w_out.shape[1]
    tiles = ncols // 512 if ncols % 512 == 0 else 1
    kc = key_cache.reshape(rb, slots * kvh, HD)
    vc = value_cache.reshape(rb, slots * kvh, HD)
    anywhere = pl.BlockSpec(memory_space=pl.ANY)
    vmem = pltpu.VMEM
    return pl.pallas_call(
        functools.partial(kernel, nb),
        out_shape=jax.ShapeDtypeStruct((rows // 2, ncols), BF16),
        in_specs=[
            pl.BlockSpec(memory_space=pltpu.SMEM),
            pl.BlockSpec(memory_space=pltpu.VMEM),
        ] + [anywhere] * 7,
        out_specs=pl.BlockSpec(memory_space=pltpu.VMEM),
        scratch_shapes=[
            vmem((rows, depth), BF16),
            vmem((nq, depth, qw), BF16),
            vmem((2, depth, 2 * HD), BF16),
            vmem((nq, qw, ncols), BF16),
            vmem((rb, slots * kvh, HD), BF16),
            vmem((rb, slots * kvh, HD), BF16),
            vmem((rows * 4, HD), F32),
            vmem((nq, rows * NH, HD), F32),
            vmem(((hid - 1) * rb * 4, HD), BF16),
            vmem((nq, (hid - 1) * rb * NH, HD), BF16),
            vmem(((hid - 1) * rb * 4, HD), BF16),
            vmem((nq, (hid - 1) * rb * NH, HD), BF16),
            vmem((rb, HD), F32),
            vmem((rb, HD), F32),
            vmem((rb, nq * NH, HD), F32),
            vmem((rb * 4, HD), F32),
            vmem((rb, nq * NH, slots * kvh), F32),
            vmem((nq, rb * NH, HD), F32),
            vmem((nq, rows * NH, HD), BF16),
            vmem((rows * NH, HD), F32),
            vmem((rows, qw), BF16),
            vmem((rows, ncols), F32),
            vmem((rows // 2, ncols), F32),
            pltpu.SemaphoreType.DMA((5 + 2 * nq,)),
            pltpu.SemaphoreType.DMA(((nq + 1) * nb,)),
            pltpu.SemaphoreType.DMA(((nq + 1) * nb,)),
            pltpu.SemaphoreType.DMA((nq * nb,)),
            pltpu.SemaphoreType.DMA((nq * nb,)),
            pltpu.SemaphoreType.DMA((tiles,)),
            pltpu.SemaphoreType.DMA((tiles,)),
        ],
        compiler_params=pltpu.CompilerParams(
            collective_id=0, has_side_effects=True, vmem_limit_bytes=56 * 1024 * 1024
        ),
    )(lengths, slot_pos, x, w_query, w_key, w_value, w_out, kc, vc)


def solution(mesh):
    placed = (
        P("groups", "hid"),
        P("hid", "ffn"),
        P("hid", "ffn"),
        P("hid", "ffn"),
        P("ffn", "hid"),
        P(("groups", "hid"), None, "ffn", None),
        P(("groups", "hid"), None, "ffn", None),
        P(("groups", "hid")),
        P(("groups", "hid"), None),
    )
    return jax.shard_map(
        functools.partial(per_device, mesh.shape["hid"]),
        mesh=mesh,
        in_specs=placed,
        out_specs=P(("groups", "ffn"), "hid"),
        check_vma=False,
    )
```

time: 179 us -> 60.4 us (0.34)
  waiting for transfers between devices: 102 us -> 0 us
  Pallas kernels: 0 us -> 58.6 us
  blocking collectives: 32.7 us -> 0 us
  matrix products: 21.5 us -> 0 us
  between operations: 14.2 us -> 0.01 us
  other arithmetic: 4.65 us -> 0 us
  local copies, waits for them, and re-layouts: 3.41 us -> 1.62 us
    unnamed x3 -> x0, waiting for transfers between devices: 94.3 us -> none
    pallas_call x0 -> x1, Pallas kernels: none -> 58.6 us  [per_device(): pl.pallas_call(functools.partial(kernel, nb), out_shape=jax.ShapeDtypeStr...]
    all_gather x1 -> x0, blocking collectives: 32.7 us -> none  [per_device(): lax.all_gather(attended, 'hid', axis=0, tiled=True)]
    dot_general x7 -> x0, matrix products: 21.5 us -> none  [the longest x1 9.43 us: per_device(): jnp.dot(lax.all_gather(attended, 'hid', axis=0, tiled=True), w_out, prefe...]
    reduce_scatter x1 -> x0, waiting for transfers between devices: 7.86 us -> none  [per_device(): lax.psum_scatter(terms, 'ffn', scatter_dimension=0, tiled=True)]
    convert_element_type x4 -> x0, other arithmetic: 2.55 us -> none  [the longest x1 1.69 us: per_device(): lax.psum_scatter(terms, 'ffn', scatter_dimension=0, tiled=True)]
    slice x2 -> x0, local copies, waits for them, and re-layouts: 1.87 us -> none  [the longest x1 1.03 us: per_device(): query = summed[:, :query_cols]]
  transfers between devices with their start and end apart: 2 -> 0, of which waited for: 2 -> 0; matrix products, arithmetic and copies ran while one was open for 0% -> 0% of each run, Pallas kernels for 0% -> 0%
where the time goes in v1:
time: 60.4 us; the launch traced here: 60.2 us
  Pallas kernels  58.6 us (97%)
  local copies, waits for them, and re-layouts  1.62 us (3%)
    pallas_call x1, Pallas kernels, per_device(): pl.pallas_call(functools.partial(kernel, nb), out_shape=jax.ShapeDtypeStr...  58.6 us
    unnamed x1, local copies, waits for them, and re-layouts  1.62 us

profile of v1, /device:TPU:0, one launch (start us, length us, event | category | flops | bytes accessed | tf_op | source)
XLA Modules:
  0.0 60.2 jit_solution(13483115513000984074)
XLA Ops:
  0.0 58.6 %shard_map.91 = bf16[48,2048]{1,0:T(8,128)(2,1)} custom-call(s32[12]{0:T(128)} %len_ref.1, s32[12,256]{1,0:T(8,128)} %slot_ref.1, bf16[96,2048]{1,0:T(8,128)(2,1)} %x_hbm.1, bf16[2048,4096]{1,0:T(8,128)(2,1)} %wq_hbm.1, bf16[2048,256]{1,0:T(8,128)(2,1)} %wk_hbm.1, bf16[2048,256]{1,0:T(8,128)(2,1)} %wv_hbm.1, bf16[4096,2048]{1,0:T(8,128)(2,1)} %wo_hbm.1, ...), custom_call_target="tpu_custom_call" | custom-call | tf_op jit(solution)/shard_map/pallas_call | solution.py:332
  58.6 1.6 %copy.11 = bf16[48,2048]{1,0:T(8,128)(2,1)} copy(bf16[48,2048]{1,0:T(8,128)(2,1)} %shard_map.91) | data formatting | bytes 393216

commit v2 on v1

--- a/solution.py
+++ b/solution.py
@@ -33,7 +33,10 @@
     rb = rows // hid
     nq = wq.shape[0]
     qw = wq.shape[2]
-    order = tuple(range(nb))
+    orders = [tuple(range(nb)), (1, 0) + tuple(range(2, nb)) if nb > 1 else (0,)]
+
+    def order_of(c):
+        return orders[(c + 1) % 2]
 
     cp_x = pltpu.make_async_copy(x_hbm, x, local_sem.at[0])
     cp_k = pltpu.make_async_copy(wk_hbm, wkv.at[0], local_sem.at[1])
@@ -77,6 +80,7 @@
         return fq.at[c - 1], sq.at[c - 1], rq.at[c - 1], rb * NH
 
     def rs_copy(c, k):
+        order = order_of(c)
         _, s, r, block = bufs(c)
         count = hid >> (k + 1)
         start = hid - (hid >> k)
@@ -88,6 +92,7 @@
         )
 
     def rs_stage(c, k):
+        order = order_of(c)
         sums, s, r, block = bufs(c)
         if k > 0:
             rs_copy(c, k - 1).wait_recv()
@@ -143,7 +148,6 @@
     pl.semaphore_wait(barrier, nb + 1)
     rs_stage(0, 0)
 
-    wave = []
     for c in range(nq):
         cp_q[c].wait()
         if c + 2 < nq:
@@ -164,10 +168,10 @@
                 fq.at[c][pl.ds(n * 2 + j, rows, stride=NH), :] = got[:, j * HD : (j + 1) * HD]
 
         rs_stage(c + 1, 0)
-        if c > 0:
-            rs_stage(c - 1, 1)
-
-    done = {(c, 0) for c in range(nq + 1)} | {(c, 1) for c in range(nq - 1)}
+        for k in range(1, min(nb, c + 1)):
+            rs_stage(c - k, k)
+
+    done = {(c - k, k) for c in range(nq) for k in range(1, min(nb, c + 1))}
     for w in range(nq + 1 + nb):
         for k in range(nb, 0, -1):
             c = w - k
@@ -234,23 +238,26 @@
             of[c, r * NH : (r + 1) * NH, :] = got[c * NH : (c + 1) * NH]
 
     block = rb * NH
-    place = 0
-    for k in range(nb):
-        place = place * 2 + my[order[k]]
+
+    def place_of(c):
+        place = 0
+        for k in range(nb):
+            place = place * 2 + my[order_of(c + 1)[k]]
+        return place
 
     def ag_copy(c, k):
-        start = lax.div(place, 1 << k) * (1 << k)
+        start = lax.div(place_of(c), 1 << k) * (1 << k)
         part = pl.ds(pl.multiple_of(start * block, block), (1 << k) * block)
         return pltpu.make_async_remote_copy(
             src_ref=ag.at[c, part], dst_ref=ag.at[c, part],
             send_sem=ag_send.at[c * nb + k], recv_sem=ag_recv.at[c * nb + k],
-            device_id={"hid": partner[order[nb - 1 - k]]}, device_id_type=MESH,
+            device_id={"hid": partner[order_of(c + 1)[nb - 1 - k]]}, device_id_type=MESH,
         )
 
-    def position_of(t):
+    def position_of(c, t):
         p = 0
         for k in range(nb):
-            p = p * 2 + ((t >> order[k]) & 1)
+            p = p * 2 + ((t >> order_of(c + 1)[k]) & 1)
         return p
 
     half = rows // 2
@@ -270,7 +277,7 @@
     def project(c):
         for t in range(hid):
             lf[t * block : (t + 1) * block, :] = ag[
-                c, position_of(t) * block : (position_of(t) + 1) * block, :
+                c, position_of(c, t) * block : (position_of(c, t) + 1) * block, :
             ].astype(F32)
         for j in range(NH):
             lhs[:, j * HD : (j + 1) * HD] = lf[pl.ds(j, rows, stride=NH), :].astype(BF16)
@@ -286,7 +293,7 @@
                 fin_copy(n).start()
 
     for c in range(nq):
-        own = pl.ds(pl.multiple_of(place * block, block), block)
+        own = pl.ds(pl.multiple_of(place_of(c) * block, block), block)
         ag[c, own, :] = of[c].astype(BF16)
         ag_copy(c, 0).start()
     for w in range(1, nq + nb):

time: 60.4 us -> 60.1 us (level)
  no operation moved by 1% of the time
where the time goes in v2:
time: 60.1 us; the launch traced here: 59.9 us
  Pallas kernels  58.2 us (97%)
  local copies, waits for them, and re-layouts  1.62 us (3%)
    pallas_call x1, Pallas kernels, per_device(): pl.pallas_call(functools.partial(kernel, nb), out_shape=jax.ShapeDtypeStr...  58.2 us
    unnamed x1, local copies, waits for them, and re-layouts  1.62 us

profile of v2, /device:TPU:0, one launch (start us, length us, event | category | flops | bytes accessed | tf_op | source)
XLA Modules:
  0.0 59.9 jit_solution(15679559877739610018)
XLA Ops:
  0.0 58.2 %shard_map.91 = bf16[48,2048]{1,0:T(8,128)(2,1)} custom-call(s32[12]{0:T(128)} %len_ref.1, s32[12,256]{1,0:T(8,128)} %slot_ref.1, bf16[96,2048]{1,0:T(8,128)(2,1)} %x_hbm.1, bf16[2048,4096]{1,0:T(8,128)(2,1)} %wq_hbm.1, bf16[2048,256]{1,0:T(8,128)(2,1)} %wk_hbm.1, bf16[2048,256]{1,0:T(8,128)(2,1)} %wv_hbm.1, bf16[4096,2048]{1,0:T(8,128)(2,1)} %wo_hbm.1, ...), custom_call_target="tpu_custom_call" | custom-call | tf_op jit(solution)/shard_map/pallas_call | solution.py:339
  58.3 1.6 %copy.11 = bf16[48,2048]{1,0:T(8,128)(2,1)} copy(bf16[48,2048]{1,0:T(8,128)(2,1)} %shard_map.91) | data formatting | bytes 393216

commit v3 on v2

--- a/solution.py
+++ b/solution.py
@@ -168,18 +168,15 @@
                 fq.at[c][pl.ds(n * 2 + j, rows, stride=NH), :] = got[:, j * HD : (j + 1) * HD]
 
         rs_stage(c + 1, 0)
-        for k in range(1, min(nb, c + 1)):
-            rs_stage(c - k, k)
-
-    done = {(c - k, k) for c in range(nq) for k in range(1, min(nb, c + 1))}
-    for w in range(nq + 1 + nb):
-        for k in range(nb, 0, -1):
-            c = w - k
-            if 0 <= c <= nq and (c, k) not in done:
-                if k == nb:
-                    rs_final(c)
-                else:
-                    rs_stage(c, k)
+        if nb > 1 and c >= 2:
+            rs_stage(c - 2, 1)
+
+    for k in range(1, nb + 1):
+        for c in range(nq + 1):
+            if k == nb:
+                rs_final(c)
+            elif k > 1 or c > nq - 3:
+                rs_stage(c, k)
 
     heads = nq * NH
     slots = slot_ref.shape[1]
@@ -296,16 +293,13 @@
         own = pl.ds(pl.multiple_of(place_of(c) * block, block), block)
         ag[c, own, :] = of[c].astype(BF16)
         ag_copy(c, 0).start()
-    for w in range(1, nq + nb):
-        for k in range(nb, 0, -1):
-            c = w - k
-            if 0 <= c < nq:
-                ag_copy(c, k - 1).wait_recv()
-                if k < nb:
-                    ag_copy(c, k).start()
-        c = w - nb
-        if 0 <= c < nq:
-            project(c)
+    for k in range(1, nb):
+        for c in range(nq):
+            ag_copy(c, k - 1).wait_recv()
+            ag_copy(c, k).start()
+    for c in range(nq):
+        ag_copy(c, nb - 1).wait_recv()
+        project(c)
 
     kept = pl.ds(pl.multiple_of(f * half, half), half)
     for n in range(tiles):

time: 60.1 us -> 42.2 us (0.70)
  Pallas kernels: 58.2 us -> 40.4 us
    pallas_call x1, Pallas kernels: 58.2 us -> 40.4 us  [per_device(): pl.pallas_call(functools.partial(kernel, nb), out_shape=jax.ShapeDtypeStr...]
where the time goes in v3:
time: 42.2 us; the launch traced here: 42 us
  Pallas kernels  40.4 us (96%)
  local copies, waits for them, and re-layouts  1.62 us (4%)
    pallas_call x1, Pallas kernels, per_device(): pl.pallas_call(functools.partial(kernel, nb), out_shape=jax.ShapeDtypeStr...  40.4 us
    unnamed x1, local copies, waits for them, and re-layouts  1.62 us

profile of v3, /device:TPU:0, one launch (start us, length us, event | category | flops | bytes accessed | tf_op | source)
XLA Modules:
  0.0 42.0 jit_solution(5060190084604831931)
XLA Ops:
  0.0 40.4 %shard_map.91 = bf16[48,2048]{1,0:T(8,128)(2,1)} custom-call(s32[12]{0:T(128)} %len_ref.1, s32[12,256]{1,0:T(8,128)} %slot_ref.1, bf16[96,2048]{1,0:T(8,128)(2,1)} %x_hbm.1, bf16[2048,4096]{1,0:T(8,128)(2,1)} %wq_hbm.1, bf16[2048,256]{1,0:T(8,128)(2,1)} %wk_hbm.1, bf16[2048,256]{1,0:T(8,128)(2,1)} %wv_hbm.1, bf16[4096,2048]{1,0:T(8,128)(2,1)} %wo_hbm.1, ...), custom_call_target="tpu_custom_call" | custom-call | tf_op jit(solution)/shard_map/pallas_call | solution.py:333
  40.4 1.6 %copy.11 = bf16[48,2048]{1,0:T(8,128)(2,1)} copy(bf16[48,2048]{1,0:T(8,128)(2,1)} %shard_map.91) | data formatting | bytes 393216
